TPU v7x, 512 devices: a whole 4x4x16 slice. The times are simulated.
512 devices in a mesh: wide: 128 (over x, y, z_hi, core), chan: 4 (over z_lo).
Axes of the slice: x: 4, y: 4, z: 16 (z_hi: 4, z_lo: 4; z = z_hi * 4 + z_lo), core: 2. Of those that a mesh axis runs over, the one named last changes fastest.
Arguments:
- activations: bfloat16 [8192, 53248], P(('wide', 'chan')), may hold values from -6 to 6
- grads: bfloat16 [8192, 16384], P(('wide', 'chan')), may hold values from -15 to 15
Outputs:
- gram: float32 [4, 256, 53248], P('chan', None, 'wide')
All inputs are finite; a program needn't handle non-finite values.
Results may differ from a plain program's by a relative error of at most 0.004.
Values may be sent and summed in bfloat16 or wider, within the bound.
A program may use at most 64 MiB of HBM per device.

v0:
```python
import math

import jax
import jax.numpy as jnp
from jax import lax
from jax.sharding import PartitionSpec as P

GROUPS = 4
SPANS = 2
ROWS = 256


def per_device(activations, grads):
    wide_count = lax.axis_size("wide")
    chan_count = lax.axis_size("chan")
    tok_local = activations.shape[0]
    features = activations.shape[1]
    tile_width = features // wide_count
    group_count = GROUPS
    all_tokens = tok_local * wide_count * chan_count
    factor = 1.0 / math.sqrt(all_tokens)
    per_group = grads.shape[1] // group_count
    squares = grads.astype(jnp.float32) ** 2
    fisher = jnp.mean(squares.reshape(tok_local, group_count, per_group), axis=2).astype(
        jnp.bfloat16
    )
    group_index = lax.axis_index("chan")
    span_len = tok_local // SPANS
    contract = (((0,), (0,)), ((), ()))
    total = jnp.zeros((ROWS, tile_width), jnp.float32)
    for number in range(SPANS):
        block = activations[number * span_len : (number + 1) * span_len]
        block_fisher = fisher[number * span_len : (number + 1) * span_len]
        window = block[:, :ROWS]
        wide_rows, wide_fisher = (
            lax.all_gather(window, "wide", axis=0, tiled=True),
            lax.all_gather(block_fisher, "wide", axis=0, tiled=True),
        )
        pieces = block.reshape(span_len, wide_count, tile_width)
        arrived = lax.all_to_all(pieces, "wide", split_axis=1, concat_axis=0, tiled=True)
        arrived = arrived.reshape(wide_count * span_len, tile_width)
        columns = lax.all_gather(arrived, "chan", axis=0, tiled=True)
        rows_all, fisher_all = (
            lax.all_gather(wide_rows, "chan", axis=0, tiled=True),
            lax.all_gather(wide_fisher, "chan", axis=0, tiled=True),
        )
        own_weight = lax.dynamic_slice_in_dim(fisher_all, group_index, 1, 1).astype(jnp.float32)
        weighted = (own_weight * rows_all.astype(jnp.float32)).astype(jnp.bfloat16)
        total = total + lax.dot_general(
            weighted, columns, contract, preferred_element_type=jnp.float32
        )
    return (total * factor).reshape(1, ROWS, tile_width)


def solution(mesh):
    in_specs = (P(("wide", "chan"), None), P(("wide", "chan"), None))
    out_specs = P("chan", None, "wide")
    return jax.shard_map(
        per_device, mesh=mesh, in_specs=in_specs, out_specs=out_specs, check_vma=False
    )
```

profile of v0, /device:TPU:64, one launch (start us, length us, event | category | flops | bytes accessed | tf_op | source)
XLA Modules:
  0.0 1098.9 jit_solution(16809078970164073557)
XLA Ops:
  6.5 1.5 fusion.8
  8.1 1.7 reshape.21
  9.8 1.6 copy.9
  11.4 20.6 %all-to-all-start = ((bf16[8,128,416]{2,0,1:T(8,128)(2,1)}), bf16[8,128,416]{2,0,1:T(8,128)(2,1)S(1)}, u32[]{:S(2)}, u32[]{:S(2)}) async-start(bf16[8,128,416]{2,0,1:T(8,128)(2,1)} %copy.9), calls=%async_computation | async-start | bytes 2097152 | tf_op jit(solution)/shard_map/all_to_all | solution.py:40
  32.0 0.0 all-gather.7.cloned.1.call-start
  32.0 0.7 fusion.7
  32.8 272.2 %all_gather.32 = bf16[1024,256]{1,0:T(8,128)(2,1)} all-gather(bf16[8,256]{1,0:T(8,128)(2,1)S(1)} %get-tuple-element.6), channel_id=1, replica_groups=mesh['wide'=128,'chan'=4] {'wide'}, dimensions={0}, use_global_device_ids=true | all-gather | bytes 528384 | tf_op jit(solution)/shard_map/all_gather | solution.py:36
  305.0 0.0 all-gather.7.cloned.1.call-update
  305.0 0.0 all-gather.9.cloned.1.call-start
  305.1 0.0 all-to-all-done
  305.1 0.0 copy-start
  305.1 1.0 copy-done
  306.1 0.0 all-gather.9.cloned.1.call-update
  306.1 0.0 copy-start.2
  306.1 1.7 reshape.23
  307.9 1.5 copy.12
  309.5 6.2 all-to-all-start.1
  315.6 0.0 all-gather.11.cloned.1.call-start
  315.7 300.0 %all_gather.37 = bf16[1024,256]{1,0:T(8,128)(2,1)} all-gather(bf16[8,256]{1,0:T(8,128)(2,1)S(1)} %get-tuple-element.5), channel_id=1, replica_groups=mesh['wide'=128,'chan'=4] {'wide'}, dimensions={0}, use_global_device_ids=true | all-gather | bytes 528384 | tf_op jit(solution)/shard_map/all_gather | solution.py:36
  615.7 0.0 all-gather.11.cloned.1.call-update
  615.8 0.2 all-gather.13.cloned.1.call-start
  616.0 0.0 all-to-all-done.1
  616.0 0.0 copy-start.1
  616.0 1.0 copy-done.1
  617.0 0.0 all-gather.13.cloned.1.call-update
  617.0 0.0 copy-done.2
  617.0 0.1 convert_multiply_fusion
  617.1 0.7 reshape.20
  617.8 0.2 reduce_sum.9
  618.0 0.1 copy.7
  618.1 221.0 %all-gather = bf16[128,8,4]{1,2,0:T(4,128)(2,1)S(1)} all-gather(bf16[1,8,4]{1,2,0:T(4,128)(2,1)S(1)} %bitcast.26), channel_id=1, replica_groups=mesh['wide'=128,'chan'=4] {'wide'}, dimensions={0}, use_global_device_ids=true | all-gather | bytes 8256 | tf_op jit(solution)/shard_map/all_gather | solution.py:37
  839.2 0.2 reshape.29
  839.4 0.1 copy.10
  839.4 217.7 %all-gather.1 = bf16[128,8,4]{1,2,0:T(4,128)(2,1)S(1)} all-gather(bf16[1,8,4]{1,2,0:T(4,128)(2,1)S(1)} %bitcast.27), channel_id=1, replica_groups=mesh['wide'=128,'chan'=4] {'wide'}, dimensions={0}, use_global_device_ids=true | all-gather | bytes 8256 | tf_op jit(solution)/shard_map/all_gather | solution.py:37
  1057.2 0.2 reshape.31
  1057.3 11.3 %all_gather.31 = bf16[4096,4]{0,1:T(4,128)(2,1)S(1)} all-gather(bf16[1024,4]{0,1:T(4,128)(2,1)S(1)} %reshape.29), channel_id=1, replica_groups=mesh['wide'=128,'chan'=4] {'chan'}, dimensions={0}, use_global_device_ids=true | all-gather | bytes 40960 | tf_op jit(solution)/shard_map/all_gather | solution.py:45
  1068.7 13.1 %all_gather.36 = bf16[4096,4]{0,1:T(4,128)(2,1)S(1)} all-gather(bf16[1024,4]{0,1:T(4,128)(2,1)S(1)} %reshape.31), channel_id=1, replica_groups=mesh['wide'=128,'chan'=4] {'chan'}, dimensions={0}, use_global_device_ids=true | all-gather | bytes 40960 | tf_op jit(solution)/shard_map/all_gather | solution.py:45
  1081.8 0.0 all-gather.7.cloned.1.call-done
  1081.9 0.0 all-gather.9.cloned.1.call-done
  1081.9 4.8 fusion
  1086.7 0.0 all-gather.11.cloned.1.call-done
  1086.8 0.0 all-gather.13.cloned.1.call-done
  1086.8 5.6 fusion.6
  (6 shorter events, 0.1 us)
Async XLA Ops:
  11.4 293.7 %all-to-all-start = ((bf16[8,128,416]{2,0,1:T(8,128)(2,1)}), bf16[8,128,416]{2,0,1:T(8,128)(2,1)S(1)}, u32[]{:S(2)}, u32[]{:S(2)}) async-start(bf16[8,128,416]{2,0,1:T(8,128)(2,1)} %copy.9), calls=%async_computation | async-start | bytes 2097152 | tf_op jit(solution)/shard_map/all_to_all | solution.py:40
  32.0 1049.9 %all-gather.7.cloned.1.call-start = ((), (), s32[]{:S(2)}) async-start(), calls=%async_computation.2 | async-start | bytes 2621440 | tf_op jit(solution)/shard_map/all_gather | solution.py:44
  305.0 776.9 %all-gather.9.cloned.1.call-start = ((), (), s32[]{:S(2)}) async-start(), calls=%async_computation.3 | async-start | bytes 5242880 | tf_op jit(solution)/shard_map/all_gather | solution.py:42
  305.1 1.0 copy-start
  306.1 310.9 %copy-start.2 = (bf16[16,16384]{1,0:T(8,128)(2,1)S(1)}, bf16[16,16384]{1,0:T(8,128)(2,1)}, u32[]{:S(2)}) copy-start(bf16[16,16384]{1,0:T(8,128)(2,1)} %param.3) | copy-start | bytes 1572868
  309.5 306.5 %all-to-all-start.1 = ((bf16[8,128,416]{2,0,1:T(8,128)(2,1)}), bf16[8,128,416]{2,0,1:T(8,128)(2,1)S(1)}, u32[]{:S(2)}, u32[]{:S(2)}) async-start(bf16[8,128,416]{2,0,1:T(8,128)(2,1)} %copy.12), calls=%async_computation.1 | async-start | bytes 2097152 | tf_op jit(solution)/shard_map/all_to_all | solution.py:40
  315.6 771.1 %all-gather.11.cloned.1.call-start = ((), (), s32[]{:S(2)}) async-start(), calls=%async_computation.4 | async-start | bytes 2621440 | tf_op jit(solution)/shard_map/all_gather | solution.py:44
  615.8 471.0 %all-gather.13.cloned.1.call-start = ((), (), s32[]{:S(2)}) async-start(), calls=%async_computation.5 | async-start | bytes 5242880 | tf_op jit(solution)/shard_map/all_gather | solution.py:42
  616.0 1.0 copy-start.1
Sparse Core Ops, SparseCore 0:
  305.1 89.5 all-gather.6
  396.8 92.6 all-gather.8
  615.9 43.0 all-gather.10
  660.9 89.9 all-gather.12
where the time goes:
time: 1100 us
  blocking collectives  1040 us (95%)
  starting transfers between devices  27.1 us (2%)
  between operations  13.3 us (1%)
  local copies, waits for them, and re-layouts  12.1 us (1%)
    all_gather x2, blocking collectives, per_device(): lax.all_gather(window, 'wide', axis=0, tiled=True)  572 us
    all_gather x2, blocking collectives, per_device(): lax.all_gather(block_fisher, 'wide', axis=0, tiled=True)  439 us
    all_to_all x2, starting transfers between devices, per_device(): lax.all_to_all(pieces, 'wide', split_axis=1, concat_axis=0, tiled=True)  26.8 us
    all_gather x2, blocking collectives, per_device(): lax.all_gather(wide_fisher, 'chan', axis=0, tiled=True)  24.4 us
  transfers between devices with their start and end apart: 6, of which 0 were waited for; matrix products, arithmetic and copies ran while one was open for 1% of the time, Pallas kernels for 0%

commit v1 on v0

v1 whole, which is shorter than its diff:
```python
import functools
import math

import jax
import jax.numpy as jnp
from jax import lax
from jax.experimental import pallas as pl
from jax.experimental.pallas import tpu as pltpu
from jax.sharding import PartitionSpec as P

MESH = pl.DeviceIdType.MESH
ROWS = 256
HALF = ROWS // 2
LANES = 128
SPAN = 4
TILE = 416
FULL = TILE // LANES
REST = TILE - FULL * LANES
PACK = LANES // REST
CHUNK = FULL * HALF + HALF // PACK


def quarter_order(group_len):
    ring = SPAN * group_len
    half = ring // 2
    first = [half] * SPAN
    for spot in range(group_len):
        order = [2, 1, 3, 0] if 2 * spot < group_len else [2, 3, 1, 0]
        for step in range(half):
            far = half - step
            for place in (spot + far, spot - far):
                slot = order.index((place // group_len) % SPAN)
                first[slot] = min(first[slot], step)
    first[3] = min(first[3], half)
    return first


def kernel(
    peers, group_len, factor,
    act, grads, out,
    gbuf, stage, win, raw, wt, prod, acc, sbuf, rbuf,
    load_sem, win_send, win_recv, raw_send, raw_recv, ring_send, ring_recv,
):
    wide = lax.axis_index("wide")
    chan = lax.axis_index("chan")
    tok = act.shape[0]
    ring = SPAN * group_len
    half = ring // 2
    core = lax.rem(wide, 2)
    run = lax.rem(lax.div(wide, 2), SPAN)
    line = lax.div(wide, 2 * SPAN)
    me = line * 2 + core
    place = run * group_len + chan

    def plane_device(peer):
        return (lax.div(peer, 2) * (2 * SPAN) + run * 2 + lax.rem(peer, 2), chan)

    def ring_device(spot):
        return (line * (2 * SPAN) + lax.div(spot, group_len) * 2 + core, lax.rem(spot, group_len))

    after = ring_device(lax.rem(place + 1, ring))
    before = ring_device(lax.rem(place + ring - 1, ring))

    barrier = pltpu.get_barrier_semaphore()

    def greet(step, carry):
        peer = lax.rem(me + step, peers)
        pl.semaphore_signal(barrier, inc=1, device_id=plane_device(peer), device_id_type=MESH)
        return carry

    load_grads = pltpu.make_async_copy(grads, gbuf, load_sem.at[0])
    load_grads.start()
    load_win = pltpu.make_async_copy(act.at[:, pl.ds(0, ROWS)], stage.at[:, pl.ds(0, ROWS)], load_sem.at[1])
    load_win.start()
    for neighbour in (after, before):
        pl.semaphore_signal(barrier, inc=1, device_id=neighbour, device_id_type=MESH)
    lax.fori_loop(1, peers, greet, 0)

    load_grads.wait()
    per_group = grads.shape[1] // group_len
    lane = lax.broadcasted_iota(jnp.int32, (tok, LANES), 1)
    weights = jnp.zeros((tok, LANES), jnp.float32)
    for group in range(group_len):
        part = gbuf[:, group * per_group : (group + 1) * per_group].astype(jnp.float32)
        mean = jnp.sum(part * part, axis=1, keepdims=True) * (1.0 / per_group)
        weights = jnp.where(lane == group, mean, weights)
    stage[:, ROWS : ROWS + LANES] = weights.astype(jnp.bfloat16)
    load_win.wait()

    pl.semaphore_wait(barrier, peers + 1)

    mine = pl.ds(pl.multiple_of(me * tok, tok), tok)

    def send_win(step, carry):
        peer = lax.rem(me + step, peers)
        pltpu.make_async_remote_copy(
            src_ref=stage, dst_ref=win.at[mine], send_sem=win_send, recv_sem=win_recv,
            device_id=plane_device(peer), device_id_type=MESH,
        ).start()
        return carry

    pltpu.make_async_copy(stage, win.at[mine], win_recv).start()
    lax.fori_loop(1, peers, send_win, 0)

    early = 2 * chan < group_len
    quarters = [
        lax.rem(run + 2, SPAN),
        lax.rem(run + jnp.where(early, 1, 3), SPAN),
        lax.rem(run + jnp.where(early, 3, 1), SPAN),
        run,
    ]

    def columns(peer, quarter):
        tile = 2 * quarter + lax.rem(peer, 2)
        block = lax.div(peer, 2) * (2 * SPAN * TILE // LANES) + FULL * tile + lax.div(tile, PACK)
        return pl.ds(pl.multiple_of(block * LANES, LANES), (FULL + 1) * LANES)

    def send_raw(slot):
        def send(step, carry):
            peer = lax.rem(me + step, peers)
            pltpu.make_async_remote_copy(
                src_ref=act.at[:, columns(peer, quarters[slot])], dst_ref=raw.at[slot, mine],
                send_sem=raw_send.at[slot], recv_sem=raw_recv.at[slot],
                device_id=plane_device(peer), device_id_type=MESH,
            ).start()
            return carry

        pltpu.make_async_copy(
            act.at[:, columns(me, quarters[slot])], raw.at[slot, mine], raw_recv.at[slot]
        ).start()
        lax.fori_loop(1, peers, send, 0)

    for slot in range(SPAN):
        send_raw(slot)

    pltpu.make_async_copy(win, win, win_recv).wait()
    turned = jnp.transpose(win[:, :ROWS].astype(jnp.float32))
    turned_weights = jnp.transpose(win[:, ROWS : ROWS + LANES].astype(jnp.float32))
    for group in range(group_len):
        wt[group] = (turned_weights[group : group + 1, :] * turned).astype(jnp.bfloat16)

    def multiply(slot):
        quarter = quarters[slot]
        skew = lax.rem(2 * quarter + core, PACK) * REST
        pltpu.make_async_copy(raw.at[slot], raw.at[slot], raw_recv.at[slot]).wait()
        place_in = lax.broadcasted_iota(jnp.int32, (HALF, LANES), 1)
        keep = place_in < LANES - skew

        def one_group(group, carry):
            prod[...] = jnp.dot(wt[group], raw[slot], preferred_element_type=jnp.float32)
            for part in range(2):
                rows = pl.ds(part * HALF, HALF)
                back = lax.rem(LANES - skew, LANES)
                turned_blocks = [
                    pltpu.roll(prod[rows, pl.ds(j * LANES, LANES)], back, 1) for j in range(FULL + 1)
                ]
                for j in range(FULL):
                    acc[quarter, group, part, pl.ds(j * HALF, HALF), :] = jnp.where(
                        keep, turned_blocks[j], turned_blocks[j + 1]
                    )
                few = HALF // PACK
                which = lax.div(lax.broadcasted_iota(jnp.int32, (few, LANES), 1), REST)
                rest = jnp.zeros((few, LANES), jnp.float32)
                for j in range(PACK):
                    piece = prod[pl.ds(part * HALF + j * few, few), pl.ds(FULL * LANES, LANES)]
                    piece = pltpu.roll(piece, lax.rem(LANES - skew + j * REST, LANES), 1)
                    rest = jnp.where(which == j, piece, rest)
                acc[quarter, group, part, pl.ds(FULL * HALF, few), :] = rest
            return carry

        lax.fori_loop(0, group_len, one_group, 0)

    need = quarter_order(group_len)

    def ring_copy(way, step, part):
        return pltpu.make_async_remote_copy(
            src_ref=sbuf.at[way, step, part], dst_ref=rbuf.at[way, step, part],
            send_sem=ring_send.at[way, step, part], recv_sem=ring_recv.at[way, step, part],
            device_id=after if way == 0 else before, device_id_type=MESH,
        )

    sent = []
    for step in range(half):
        for slot in range(SPAN):
            if need[slot] == step:
                multiply(slot)
        far = half - step
        for part in range(2):
            for way in range(2):
                if step == 0 and way != part:
                    continue
                goal = lax.rem(place + far if way == 0 else place + ring - far, ring)
                total = acc[lax.div(goal, group_len), lax.rem(goal, group_len), part]
                if step > 1 or (step == 1 and way == part):
                    ring_copy(way, step - 1, part).wait_recv()
                    total = total + rbuf[way, step - 1, part].astype(jnp.float32)
                sbuf[way, step, part] = total.astype(jnp.bfloat16)
                copy = ring_copy(way, step, part)
                copy.start()
                sent.append(copy)
    for slot in range(SPAN):
        if need[slot] == half:
            multiply(slot)

    for part in range(2):
        total = acc[run, chan, part]
        for way in range(2):
            ring_copy(way, half - 1, part).wait_recv()
            total = total + rbuf[way, half - 1, part].astype(jnp.float32)
        total = total * factor
        for j in range(FULL):
            out[0, pl.ds(part * HALF, HALF), pl.ds(j * LANES, LANES)] = total[j * HALF : (j + 1) * HALF]
        few = HALF // PACK
        rest = total[FULL * HALF :]
        for j in range(PACK):
            piece = pltpu.roll(rest, (LANES - j * REST) % LANES, 1)
            out[0, pl.ds(part * HALF + j * few, few), pl.ds(FULL * LANES, REST)] = piece[:, :REST]

    for copy in sent:
        copy.wait_send()
    others = pl.ds(0, (peers - 1) * tok)
    pltpu.make_async_copy(win.at[others], win.at[others], win_send).wait()
    for slot in range(SPAN):
        pltpu.make_async_copy(raw.at[slot, others], raw.at[slot, others], raw_send.at[slot]).wait()


def solution(mesh):
    wide, group_len = mesh.shape["wide"], mesh.shape["chan"]
    peers = wide // SPAN
    half = SPAN * group_len // 2

    def step(activations, grads):
        tok = activations.shape[0]
        plane = peers * tok
        factor = 1.0 / math.sqrt(plane * SPAN * group_len)
        return pl.pallas_call(
            functools.partial(kernel, peers, group_len, factor),
            out_shape=jax.ShapeDtypeStruct((1, ROWS, TILE), jnp.float32),
            in_specs=[pl.BlockSpec(memory_space=pl.ANY)] * 2,
            out_specs=pl.BlockSpec(memory_space=pltpu.VMEM),
            scratch_shapes=[
                pltpu.VMEM(grads.shape, jnp.bfloat16),
                pltpu.VMEM((tok, ROWS + LANES), jnp.bfloat16),
                pltpu.VMEM((plane, ROWS + LANES), jnp.bfloat16),
                pltpu.VMEM((SPAN, plane, (FULL + 1) * LANES), jnp.bfloat16),
                pltpu.VMEM((group_len, ROWS, plane), jnp.bfloat16),
                pltpu.VMEM((ROWS, (FULL + 1) * LANES), jnp.float32),
                pltpu.VMEM((SPAN, group_len, 2, CHUNK, LANES), jnp.float32),
                pltpu.VMEM((2, half, 2, CHUNK, LANES), jnp.bfloat16),
                pltpu.VMEM((2, half, 2, CHUNK, LANES), jnp.bfloat16),
                pltpu.SemaphoreType.DMA((2,)),
                pltpu.SemaphoreType.DMA,
                pltpu.SemaphoreType.DMA,
                pltpu.SemaphoreType.DMA((SPAN,)),
                pltpu.SemaphoreType.DMA((SPAN,)),
                pltpu.SemaphoreType.DMA((2, half, 2)),
                pltpu.SemaphoreType.DMA((2, half, 2)),
            ],
            compiler_params=pltpu.CompilerParams(
                collective_id=0, has_side_effects=True, vmem_limit_bytes=48 * 1024 * 1024
            ),
        )(activations, grads)

    return jax.shard_map(
        step,
        mesh=mesh,
        in_specs=(P(("wide", "chan"), None), P(("wide", "chan"), None)),
        out_specs=P("chan", None, "wide"),
        check_vma=False,
    )
```

time: 1100 us -> 84.5 us (0.08)
  the two profiles are of different devices: /device:TPU:64 before, /device:TPU:2 now
where the time goes in v1:
time: 84.5 us; the launch traced here: 84.3 us
  Pallas kernels  80.9 us (96%)
  local copies, waits for them, and re-layouts  3.43 us (4%)
    pallas_call x1, Pallas kernels, step(): pl.pallas_call(functools.partial(kernel, peers, group_len, factor), out_s...  80.9 us
    unnamed x4, local copies, waits for them, and re-layouts  2.49 us

profile of v1, /device:TPU:2, one launch (start us, length us, event | category | flops | bytes accessed | tf_op | source)
XLA Modules:
  0.0 84.3 jit_solution(3632914304956793778)
XLA Ops:
  0.0 0.0 copy-start
  0.0 1.5 %copy-done = bf16[16,53248]{1,0:T(8,128)(2,1)S(1)} copy-done((bf16[16,53248]{1,0:T(8,128)(2,1)S(1)}, bf16[16,53248]{1,0:T(8,128)(2,1)}, u32[]{:S(2)}) %copy-start) | copy-done | bytes 1703960
  1.5 0.0 copy-start.1
  1.5 1.0 %copy-done.1 = bf16[16,16384]{1,0:T(8,128)(2,1)S(1)} copy-done((bf16[16,16384]{1,0:T(8,128)(2,1)S(1)}, bf16[16,16384]{1,0:T(8,128)(2,1)}, u32[]{:S(2)}) %copy-start.1) | copy-done | bytes 524312
  2.5 80.9 %shard_map.28 = f32[1,256,416]{2,1,0:T(8,128)S(1)} custom-call(bf16[16,53248]{1,0:T(8,128)(2,1)S(1)} %copy-done, bf16[16,16384]{1,0:T(8,128)(2,1)S(1)} %copy-done.1), custom_call_target="tpu_custom_call" | custom-call | tf_op jit(solution)/shard_map/pallas_call | solution.py:236
  83.4 0.9 %copy.3 = f32[1,256,416]{1,2,0:T(8,128)} copy(f32[1,256,416]{2,1,0:T(8,128)S(1)} %shard_map.28) | data formatting | bytes 851968 | tf_op jit(solution)/shard_map/pallas_call | solution.py:236
Async XLA Ops:
  0.0 1.5 %copy-start = (bf16[16,53248]{1,0:T(8,128)(2,1)S(1)}, bf16[16,53248]{1,0:T(8,128)(2,1)}, u32[]{:S(2)}) copy-start(bf16[16,53248]{1,0:T(8,128)(2,1)} %act.1) | copy-start | bytes 5111812
  1.5 1.0 %copy-start.1 = (bf16[16,16384]{1,0:T(8,128)(2,1)S(1)}, bf16[16,16384]{1,0:T(8,128)(2,1)}, u32[]{:S(2)}) copy-start(bf16[16,16384]{1,0:T(8,128)(2,1)} %grads.1) | copy-start | bytes 1572868

commit v2 on v1

v2 whole, which is shorter than its diff:
```python
import functools
import math

import jax
import jax.numpy as jnp
from jax import lax
from jax.experimental import pallas as pl
from jax.experimental.pallas import tpu as pltpu
from jax.sharding import PartitionSpec as P

MESH = pl.DeviceIdType.MESH
ROWS = 256
LANES = 128
SPAN = 4
TILE = 416
FULL = TILE // LANES
MAIN = FULL * LANES
REST = TILE - MAIN
PACK = LANES // REST
FEW = ROWS // PACK
BLOCK = MAIN // LANES * ROWS + FEW
PARTS = 2
PART = ROWS // PARTS
CHUNK = FULL * PART
WHERE = [pl.ds(part * CHUNK, CHUNK) for part in range(PARTS)] + [pl.ds(PARTS * CHUNK, FEW)]
LAST = PARTS
AT = [[0, 1, 2], [3, 4, 5], [6, 7, 8], [10, 11, 12]]
AT_LAST = 9
MESSAGES = [(0, 3), (3, 3), (6, 4), (10, 3)]
BLOCKS = 13
LINE = 2 * SPAN * TILE // LANES
WIDTH = 4
STRIDE = 5


def first_steps(group_len):
    ring = SPAN * group_len
    half = ring // 2
    table = []
    for spot in range(group_len):
        order = [2, 1, 3, 0] if 2 * spot < group_len else [2, 3, 1, 0]
        first = [half] * SPAN
        for step in range(half):
            far = half - step
            for place in (spot + far, spot - far):
                slot = order.index((place // group_len) % SPAN)
                first[slot] = min(first[slot], step)
        table.append(first)
    return table


def kernel(
    peers, group_len, factor,
    act_hbm, grads_hbm, out,
    gbuf, act, head, packed, win, raw, wt, own, own_last, sbuf, rbuf,
    load_sem, win_send, win_recv, raw_send, raw_recv, ring_send, ring_recv,
):
    wide = lax.axis_index("wide")
    chan = lax.axis_index("chan")
    tok = act.shape[0]
    ring = SPAN * group_len
    half = ring // 2
    lines = peers // 2
    rows_y = 4 if lines % 4 == 0 else 1
    rows_x = lines // rows_y
    core = lax.rem(wide, 2)
    run = lax.rem(lax.div(wide, 2), SPAN)
    line = lax.div(wide, 2 * SPAN)
    me = line * 2 + core
    lead = core * lines + line
    place = run * group_len + chan
    width = min(WIDTH, peers)

    def plane_device(spot, side):
        return (spot * (2 * SPAN) + run * 2 + side, chan)

    def ring_device(spot):
        return (line * (2 * SPAN) + lax.div(spot, group_len) * 2 + core, lax.rem(spot, group_len))

    all_x = [lax.rem(lax.div(line, rows_y) + step, rows_x) for step in range(rows_x)]
    all_y = [lax.rem(line + step, rows_y) for step in range(rows_y)]
    other_lines = []
    for step in range(1, lines):
        step = step * STRIDE % lines
        other_lines.append(all_x[step // rows_y] * rows_y + all_y[step % rows_y])
    twin = 1 - core
    peer_list = [(spot, side) for spot in other_lines for side in (core, twin)] + [(line, twin)]

    after = ring_device(lax.rem(place + 1, ring))
    before = ring_device(lax.rem(place + ring - 1, ring))

    barrier = pltpu.get_barrier_semaphore()

    load_grads = pltpu.make_async_copy(grads_hbm, gbuf, load_sem.at[0])
    load_grads.start()
    load_act = pltpu.make_async_copy(act_hbm, act, load_sem.at[1])
    load_act.start()
    for neighbour in (after, before):
        pl.semaphore_signal(barrier, inc=1, device_id=neighbour, device_id_type=MESH)
    for spot, side in peer_list:
        pl.semaphore_signal(barrier, inc=1, device_id=plane_device(spot, side), device_id_type=MESH)

    load_grads.wait()
    per_group = gbuf.shape[1] // group_len
    lane = lax.broadcasted_iota(jnp.int32, (tok, LANES), 1)
    weights = jnp.zeros((tok, LANES), jnp.float32)
    for group in range(group_len):
        part = gbuf[:, group * per_group : (group + 1) * per_group].astype(jnp.float32)
        mean = jnp.sum(part * part, axis=1, keepdims=True) * (1.0 / per_group)
        weights = jnp.where(lane == group, mean, weights)
    weights = weights.astype(jnp.bfloat16)
    load_act.wait()
    head[:, :ROWS] = act[:, :ROWS]
    head[:, ROWS:] = weights

    early = 2 * chan < group_len
    quarters = [
        lax.rem(run + 2, SPAN),
        lax.rem(run + jnp.where(early, 1, 3), SPAN),
        lax.rem(run + jnp.where(early, 3, 1), SPAN),
        run,
    ]

    def slot_of(quarter):
        ahead = lax.rem(quarter + SPAN - run, SPAN)
        one = jnp.where(early, 1, 2)
        return jnp.where(ahead == 2, 0, jnp.where(ahead == 0, 3, jnp.where(ahead == 1, one, 3 - one)))

    def block_of(peer, quarter):
        tile = 2 * quarter + lax.rem(peer, 2)
        block = lax.div(peer, 2) * LINE + FULL * tile + lax.div(tile, PACK)
        return block, lax.rem(tile, PACK) * REST

    def lanes(block):
        return pl.ds(pl.multiple_of(block * LANES, LANES), LANES)

    def turn(value, shift):
        return pltpu.roll(value, lax.rem(shift + LANES, LANES), 1)

    def fill(message):
        first, count = MESSAGES[message]

        def some(group, carry):
            for number in range(width):
                peer = group * width + number
                for slot in range(SPAN):
                    wanted = [j for j in range(FULL) if first <= AT[slot][j] < first + count]
                    if not wanted:
                        continue
                    block, skew = block_of(peer, quarters[slot])
                    turned = {
                        j: turn(act[:, lanes(block + j)], -skew) for j in range(wanted[0], wanted[-1] + 2)
                    }
                    for j in wanted:
                        packed[peer, :, AT[slot][j] * LANES : (AT[slot][j] + 1) * LANES] = jnp.where(
                            lane < LANES - skew, turned[j], turned[j + 1]
                        )
                if first <= AT_LAST < first + count:
                    rest = jnp.zeros((tok, LANES), jnp.bfloat16)
                    for slot in range(SPAN):
                        block, skew = block_of(peer, quarters[slot])
                        piece = turn(act[:, lanes(block + FULL)], slot * REST - skew)
                        rest = jnp.where(lax.div(lane, REST) == slot, piece, rest)
                    packed[peer, :, AT_LAST * LANES : (AT_LAST + 1) * LANES] = rest
            return carry

        lax.fori_loop(0, peers // width, some, 0)

    fill(0)

    pl.semaphore_wait(barrier, peers + 1)

    mine = pl.ds(pl.multiple_of(lead * tok, tok), tok)
    side_rows = pl.ds(pl.multiple_of(core * lines * tok, tok), lines * tok)
    twin_rows = pl.ds(pl.multiple_of(twin * lines * tok, tok), lines * tok)

    def send_head():
        pltpu.make_async_copy(head, win.at[mine], win_recv.at[0]).start()
        for spot in other_lines:
            pltpu.make_async_remote_copy(
                src_ref=head, dst_ref=win.at[mine], send_sem=win_send.at[0], recv_sem=win_recv.at[0],
                device_id=plane_device(spot, core), device_id_type=MESH,
            ).start()

    def size_of(message):
        first, count = MESSAGES[message]
        return pl.ds(first * LANES, count * LANES)

    def send_raw(message):
        size = size_of(message)
        pltpu.make_async_copy(packed.at[me, :, size], raw.at[mine, size], raw_recv.at[message]).start()
        for spot, side in peer_list:
            pltpu.make_async_remote_copy(
                src_ref=packed.at[spot * 2 + side, :, size], dst_ref=raw.at[mine, size],
                send_sem=raw_send.at[message], recv_sem=raw_recv.at[message],
                device_id=plane_device(spot, side), device_id_type=MESH,
            ).start()

    def take_raw(message):
        all_of = raw.at[:, size_of(message)]
        pltpu.make_async_copy(all_of, all_of, raw_recv.at[message]).wait()

    send_head()
    send_raw(0)
    pltpu.make_async_copy(win.at[side_rows], win.at[side_rows], win_recv.at[0]).wait()
    hand_over = pltpu.make_async_remote_copy(
        src_ref=win.at[side_rows], dst_ref=win.at[side_rows], send_sem=win_send.at[1], recv_sem=win_recv.at[1],
        device_id=plane_device(line, twin), device_id_type=MESH,
    )
    hand_over.start()
    fill(1)
    send_raw(1)
    fill(2)
    fill(3)

    pltpu.make_async_copy(win.at[twin_rows], win.at[twin_rows], win_recv.at[1]).wait()

    turned_rows = jnp.transpose(win[:, :ROWS].astype(jnp.float32))
    turned_weights = jnp.transpose(win[:, ROWS : ROWS + LANES].astype(jnp.float32))
    for group in range(group_len):
        wt[group] = (turned_weights[group : group + 1, :] * turned_rows).astype(jnp.bfloat16)

    table = first_steps(group_len)
    third = min(table[spot][2] for spot in range(group_len))

    def take_at(step):
        for slot in range(SPAN):
            spots = [spot for spot in range(group_len) if table[spot][slot] == step]
            if slot == 2:
                spots = list(range(group_len)) if step == third else []
            if len(spots) == group_len:
                take_raw(slot)
            elif spots:
                hit = chan == spots[0]
                for spot in spots[1:]:
                    hit = jnp.logical_or(hit, chan == spot)
                pl.when(hit)(functools.partial(take_raw, slot))

    few_lane = lax.div(lax.broadcasted_iota(jnp.int32, (FEW, LANES), 1), REST)

    def choose(slot, values):
        picked = values[-1]
        for number in range(SPAN - 1):
            picked = jnp.where(slot == number, values[number], picked)
        return picked

    def multiply(way, step, goal, first, count):
        slot = slot_of(lax.div(goal, group_len))
        start = pl.multiple_of(choose(slot, [AT[number][first] for number in range(SPAN)]) * LANES, LANES)
        main = jnp.dot(
            wt[lax.rem(goal, group_len)], raw[:, pl.ds(start, count * LANES)], preferred_element_type=jnp.float32
        )
        for part in range(PARTS):
            for j in range(count):
                top = part * CHUNK + (first + j) * PART
                own[way, step, top : top + PART] = main[
                    part * PART : (part + 1) * PART, j * LANES : (j + 1) * LANES
                ]

    def multiply_last():
        for group in range(group_len):
            last = jnp.dot(
                wt[group], raw[:, AT_LAST * LANES : (AT_LAST + 1) * LANES], preferred_element_type=jnp.float32
            )
            for slot in range(SPAN):
                rest = jnp.zeros((FEW, LANES), jnp.float32)
                for j in range(PACK):
                    piece = last[j * FEW : (j + 1) * FEW]
                    shift = (j - slot) % PACK * REST
                    rest = jnp.where(few_lane == j, pltpu.roll(piece, shift, 1) if shift else piece, rest)
                own_last[slot, group] = rest

    def ring_copy(way, step, part):
        return pltpu.make_async_remote_copy(
            src_ref=sbuf.at[way, step, WHERE[part]], dst_ref=rbuf.at[way, step, WHERE[part]],
            send_sem=ring_send.at[way, step, part], recv_sem=ring_recv.at[way, step, part],
            device_id=after if way == 0 else before, device_id_type=MESH,
        )

    parts = list(range(PARTS))
    opening = [parts[: PARTS // 2], parts[PARTS // 2 :] + [LAST]]
    orders = [parts[PARTS // 2 :] + parts[: PARTS // 2], parts]

    def goal_of(way, step):
        far = half - step
        return lax.rem(place + far if way == 0 else place + ring - far, ring)

    def own_part(way, step, part, goal):
        if part == LAST:
            return own_last[slot_of(lax.div(goal, group_len)), lax.rem(goal, group_len)]
        return own[way, step, WHERE[part]]

    sent = []

    def pass_on(step, last):
        for number in range(1 if last else PARTS):
            for way in range(2):
                part = LAST if last else orders[way][number]
                if step == 0 and part not in opening[way]:
                    continue
                total = own_part(way if step else 0, step, part, goal_of(way, step))
                if step > 1 or (step == 1 and part in opening[way]):
                    ring_copy(way, step - 1, part).wait_recv()
                    total = total + rbuf[way, step - 1, WHERE[part]].astype(jnp.float32)
                sbuf[way, step, WHERE[part]] = total.astype(jnp.bfloat16)
                copy = ring_copy(way, step, part)
                copy.start()
                sent.append(copy)

    def prepare(step, first, count):
        if step == half:
            multiply(1, 0, place, first, count)
            return
        for way in range(1 if step == 0 else 2):
            multiply(way, step, goal_of(way, step), first, count)

    done = 0
    for step in range(half + 1):
        take_at(step)
        prepare(step, 0, FULL)
        if step == half:
            break
        if step == third:
            multiply_last()
        for late in range(2):
            if step >= third and done <= step:
                pass_on(done, True)
                done += 1
            if late == 0:
                pass_on(step, False)
        if step < 2:
            send_raw(2 + step)
    while done < half:
        pass_on(done, True)
        done += 1

    for part in parts + [LAST]:
        total = own_part(1, 0, part, place)
        for way in range(2):
            ring_copy(way, half - 1, part).wait_recv()
            total = total + rbuf[way, half - 1, WHERE[part]].astype(jnp.float32)
        total = jnp.transpose(total * factor)
        if part == LAST:
            for j in range(PACK):
                out[0, MAIN:TILE, j * FEW : (j + 1) * FEW] = total[j * REST : (j + 1) * REST]
        else:
            for j in range(FULL):
                out[0, j * LANES : (j + 1) * LANES, part * PART : (part + 1) * PART] = total[
                    :, j * PART : (j + 1) * PART
                ]

    for copy in sent:
        copy.wait_send()
    others = pl.ds(0, (peers - 1) * tok)
    hand_over.wait_send()
    half_others = pl.ds(0, (lines - 1) * tok)
    if lines > 1:
        pltpu.make_async_copy(win.at[half_others], win.at[half_others], win_send.at[0]).wait()
    for message in range(len(MESSAGES)):
        sent_of = raw.at[others, size_of(message)]
        pltpu.make_async_copy(sent_of, sent_of, raw_send.at[message]).wait()


def solution(mesh):
    wide, group_len = mesh.shape["wide"], mesh.shape["chan"]
    peers = wide // SPAN
    half = SPAN * group_len // 2

    def step(activations, grads):
        tok = activations.shape[0]
        plane = peers * tok
        factor = 1.0 / math.sqrt(plane * SPAN * group_len)
        gram = pl.pallas_call(
            functools.partial(kernel, peers, group_len, factor),
            out_shape=jax.ShapeDtypeStruct((1, TILE, ROWS), jnp.float32),
            in_specs=[pl.BlockSpec(memory_space=pltpu.HBM)] * 2,
            out_specs=pl.BlockSpec(memory_space=pltpu.VMEM),
            scratch_shapes=[
                pltpu.VMEM(grads.shape, jnp.bfloat16),
                pltpu.VMEM(activations.shape, jnp.bfloat16),
                pltpu.VMEM((tok, ROWS + LANES), jnp.bfloat16),
                pltpu.VMEM((peers, tok, BLOCKS * LANES), jnp.bfloat16),
                pltpu.VMEM((plane, ROWS + LANES), jnp.bfloat16),
                pltpu.VMEM((plane, BLOCKS * LANES), jnp.bfloat16),
                pltpu.VMEM((group_len, ROWS, plane), jnp.bfloat16),
                pltpu.VMEM((2, half, BLOCK, LANES), jnp.float32),
                pltpu.VMEM((SPAN, group_len, FEW, LANES), jnp.float32),
                pltpu.VMEM((2, half, BLOCK, LANES), jnp.bfloat16),
                pltpu.VMEM((2, half, BLOCK, LANES), jnp.bfloat16),
                pltpu.SemaphoreType.DMA((2,)),
                pltpu.SemaphoreType.DMA((2,)),
                pltpu.SemaphoreType.DMA((2,)),
                pltpu.SemaphoreType.DMA((len(MESSAGES),)),
                pltpu.SemaphoreType.DMA((len(MESSAGES),)),
                pltpu.SemaphoreType.DMA((2, half, LAST + 1)),
                pltpu.SemaphoreType.DMA((2, half, LAST + 1)),
            ],
            compiler_params=pltpu.CompilerParams(
                collective_id=0, has_side_effects=True, vmem_limit_bytes=62 * 1024 * 1024
            ),
        )(activations, grads)
        return jnp.transpose(gram, (0, 2, 1))

    return jax.shard_map(
        step,
        mesh=mesh,
        in_specs=(P(("wide", "chan"), None), P(("wide", "chan"), None)),
        out_specs=P("chan", None, "wide"),
        check_vma=False,
    )
```

time: 84.5 us -> 73 us (0.86)
  Pallas kernels: 80.9 us -> 71 us
  local copies, waits for them, and re-layouts: 3.43 us -> 1.79 us
    pallas_call x1, Pallas kernels: 80.9 us -> 71 us  [step(): pl.pallas_call(functools.partial(kernel, peers, group_len, factor), out_s...]
    pallas_call x1 -> x0, local copies, waits for them, and re-layouts: 0.93 us -> none  [step(): pl.pallas_call(functools.partial(kernel, peers, group_len, factor), out_s...]
    unnamed x4 -> x1, local copies, waits for them, and re-layouts: 2.49 us -> 1.79 us
where the time goes in v2:
time: 73 us; the launch traced here: 72.8 us
  Pallas kernels  71 us (97%)
  local copies, waits for them, and re-layouts  1.79 us (2%)
    pallas_call x1, Pallas kernels, step(): pl.pallas_call(functools.partial(kernel, peers, group_len, factor), out_s...  71 us
    unnamed x1, local copies, waits for them, and re-layouts  1.79 us

profile of v2, /device:TPU:2, one launch (start us, length us, event | category | flops | bytes accessed | tf_op | source)
XLA Modules:
  0.0 72.8 jit_solution(8019852022941112612)
XLA Ops:
  0.0 71.0 %shard_map.28 = f32[1,416,256]{2,1,0:T(8,128)} custom-call(bf16[16,53248]{1,0:T(8,128)(2,1)} %act_hbm.1, bf16[16,16384]{1,0:T(8,128)(2,1)} %grads_hbm.1), custom_call_target="tpu_custom_call" | custom-call | tf_op jit(solution)/shard_map/pallas_call | solution.py:373
  71.0 1.8 %copy.4 = f32[1,256,416]{1,2,0:T(8,128)} copy(f32[1,256,416]{1,2,0:T(8,128)} %bitcast.1) | data formatting | bytes 851968

commit v3 on v2

--- a/solution.py
+++ b/solution.py
@@ -19,14 +19,12 @@
 PACK = LANES // REST
 FEW = ROWS // PACK
 BLOCK = MAIN // LANES * ROWS + FEW
-PARTS = 2
-PART = ROWS // PARTS
-CHUNK = FULL * PART
-WHERE = [pl.ds(part * CHUNK, CHUNK) for part in range(PARTS)] + [pl.ds(PARTS * CHUNK, FEW)]
-LAST = PARTS
-AT = [[0, 1, 2], [3, 4, 5], [6, 7, 8], [10, 11, 12]]
+HALF = ROWS // 2
+WHERE = [pl.ds(part * HALF, HALF) for part in range(2 * FULL)] + [pl.ds(FULL * ROWS, FEW)]
+LAST = 2 * FULL
+AT = [[0, 2, 3], [1, 4, 5], [6, 7, 8], [10, 11, 12]]
 AT_LAST = 9
-MESSAGES = [(0, 3), (3, 3), (6, 4), (10, 3)]
+MESSAGES = [(0, 2), (2, 2), (4, 2), (6, 4), (10, 3)]
 BLOCKS = 13
 LINE = 2 * SPAN * TILE // LANES
 WIDTH = 4
@@ -202,16 +200,17 @@
 
     send_head()
     send_raw(0)
+    for message in (1, 2):
+        fill(message)
+        send_raw(message)
     pltpu.make_async_copy(win.at[side_rows], win.at[side_rows], win_recv.at[0]).wait()
     hand_over = pltpu.make_async_remote_copy(
         src_ref=win.at[side_rows], dst_ref=win.at[side_rows], send_sem=win_send.at[1], recv_sem=win_recv.at[1],
         device_id=plane_device(line, twin), device_id_type=MESH,
     )
     hand_over.start()
-    fill(1)
-    send_raw(1)
-    fill(2)
     fill(3)
+    fill(4)
 
     pltpu.make_async_copy(win.at[twin_rows], win.at[twin_rows], win_recv.at[1]).wait()
 
@@ -223,18 +222,14 @@
     table = first_steps(group_len)
     third = min(table[spot][2] for spot in range(group_len))
 
-    def take_at(step):
-        for slot in range(SPAN):
-            spots = [spot for spot in range(group_len) if table[spot][slot] == step]
-            if slot == 2:
-                spots = list(range(group_len)) if step == third else []
-            if len(spots) == group_len:
-                take_raw(slot)
-            elif spots:
-                hit = chan == spots[0]
-                for spot in spots[1:]:
-                    hit = jnp.logical_or(hit, chan == spot)
-                pl.when(hit)(functools.partial(take_raw, slot))
+    def take_fourth(step):
+        spots = [spot for spot in range(group_len) if table[spot][3] == step]
+        if not spots:
+            return
+        hit = chan == spots[0]
+        for spot in spots[1:]:
+            hit = jnp.logical_or(hit, chan == spot)
+        pl.when(hit)(lambda: take_raw(4))
 
     few_lane = lax.div(lax.broadcasted_iota(jnp.int32, (FEW, LANES), 1), REST)
 
@@ -250,12 +245,8 @@
         main = jnp.dot(
             wt[lax.rem(goal, group_len)], raw[:, pl.ds(start, count * LANES)], preferred_element_type=jnp.float32
         )
-        for part in range(PARTS):
-            for j in range(count):
-                top = part * CHUNK + (first + j) * PART
-                own[way, step, top : top + PART] = main[
-                    part * PART : (part + 1) * PART, j * LANES : (j + 1) * LANES
-                ]
+        for j in range(count):
+            own[way, step, (first + j) * ROWS : (first + j + 1) * ROWS] = main[:, j * LANES : (j + 1) * LANES]
 
     def multiply_last():
         for group in range(group_len):
@@ -277,9 +268,7 @@
             device_id=after if way == 0 else before, device_id_type=MESH,
         )
 
-    parts = list(range(PARTS))
-    opening = [parts[: PARTS // 2], parts[PARTS // 2 :] + [LAST]]
-    orders = [parts[PARTS // 2 :] + parts[: PARTS // 2], parts]
+    opening = [[0, 2, 4], [1, 3, 5, LAST]]
 
     def goal_of(way, step):
         far = half - step
@@ -292,20 +281,22 @@
 
     sent = []
 
-    def pass_on(step, last):
-        for number in range(1 if last else PARTS):
-            for way in range(2):
-                part = LAST if last else orders[way][number]
-                if step == 0 and part not in opening[way]:
-                    continue
-                total = own_part(way if step else 0, step, part, goal_of(way, step))
-                if step > 1 or (step == 1 and part in opening[way]):
-                    ring_copy(way, step - 1, part).wait_recv()
-                    total = total + rbuf[way, step - 1, WHERE[part]].astype(jnp.float32)
-                sbuf[way, step, WHERE[part]] = total.astype(jnp.bfloat16)
-                copy = ring_copy(way, step, part)
-                copy.start()
-                sent.append(copy)
+    def pass_on(step, blocks):
+        for block in blocks:
+            pair = [LAST] if block == FULL else [2 * block, 2 * block + 1]
+            for number in range(len(pair)):
+                for way in range(2):
+                    part = pair[number if way else len(pair) - 1 - number]
+                    if step == 0 and part not in opening[way]:
+                        continue
+                    total = own_part(way if step else 0, step, part, goal_of(way, step))
+                    if step > 1 or (step == 1 and part in opening[way]):
+                        ring_copy(way, step - 1, part).wait_recv()
+                        total = total + rbuf[way, step - 1, WHERE[part]].astype(jnp.float32)
+                    sbuf[way, step, WHERE[part]] = total.astype(jnp.bfloat16)
+                    copy = ring_copy(way, step, part)
+                    copy.start()
+                    sent.append(copy)
 
     def prepare(step, first, count):
         if step == half:
@@ -314,40 +305,57 @@
         for way in range(1 if step == 0 else 2):
             multiply(way, step, goal_of(way, step), first, count)
 
+    take_raw(0)
+    prepare(0, 0, 1)
+    pass_on(0, [0])
+    prepare(1, 0, 1)
+    pass_on(1, [0])
+    take_raw(1)
+    prepare(0, 1, 2)
+    pass_on(0, [1, 2])
+    send_raw(3)
+    take_raw(2)
+    prepare(1, 1, 2)
+    pass_on(1, [1, 2])
+    send_raw(4)
     done = 0
-    for step in range(half + 1):
-        take_at(step)
-        prepare(step, 0, FULL)
+    taken = False
+    for step in range(2, half + 1):
+        if step >= third and not taken:
+            take_raw(3)
+            taken = True
+            multiply_last()
+            for earlier in range(step):
+                take_fourth(earlier)
+        take_fourth(step)
+        prepare(step, 0, 1)
+        prepare(step, 1, 2)
         if step == half:
             break
-        if step == third:
-            multiply_last()
-        for late in range(2):
-            if step >= third and done <= step:
-                pass_on(done, True)
-                done += 1
-            if late == 0:
-                pass_on(step, False)
-        if step < 2:
-            send_raw(2 + step)
+        if taken and done <= step:
+            pass_on(done, [FULL])
+            done += 1
+        pass_on(step, [0, 1, 2])
+        if taken and done <= step:
+            pass_on(done, [FULL])
+            done += 1
     while done < half:
-        pass_on(done, True)
+        pass_on(done, [FULL])
         done += 1
 
-    for part in parts + [LAST]:
-        total = own_part(1, 0, part, place)
-        for way in range(2):
-            ring_copy(way, half - 1, part).wait_recv()
-            total = total + rbuf[way, half - 1, WHERE[part]].astype(jnp.float32)
-        total = jnp.transpose(total * factor)
-        if part == LAST:
-            for j in range(PACK):
-                out[0, MAIN:TILE, j * FEW : (j + 1) * FEW] = total[j * REST : (j + 1) * REST]
-        else:
-            for j in range(FULL):
-                out[0, j * LANES : (j + 1) * LANES, part * PART : (part + 1) * PART] = total[
-                    :, j * PART : (j + 1) * PART
-                ]
+    for block in range(FULL + 1):
+        for part in [LAST] if block == FULL else [2 * block, 2 * block + 1]:
+            total = own_part(1, 0, part, place)
+            for way in range(2):
+                ring_copy(way, half - 1, part).wait_recv()
+                total = total + rbuf[way, half - 1, WHERE[part]].astype(jnp.float32)
+            total = jnp.transpose(total * factor)
+            if part == LAST:
+                for j in range(PACK):
+                    out[0, MAIN:TILE, j * FEW : (j + 1) * FEW] = total[j * REST : (j + 1) * REST]
+            else:
+                side = part % 2 * HALF
+                out[0, block * LANES : (block + 1) * LANES, side : side + HALF] = total
 
     for copy in sent:
         copy.wait_send()
@@ -396,7 +404,7 @@
                 pltpu.SemaphoreType.DMA((2, half, LAST + 1)),
             ],
             compiler_params=pltpu.CompilerParams(
-                collective_id=0, has_side_effects=True, vmem_limit_bytes=62 * 1024 * 1024
+                collective_id=0, has_side_effects=True, vmem_limit_bytes=53 * 1024 * 1024
             ),
         )(activations, grads)
         return jnp.transpose(gram, (0, 2, 1))

time: 73 us -> 74 us (1.014)
  the two profiles are of different devices: /device:TPU:2 before, /device:TPU:6 now
where the time goes in v3:
time: 74 us; the launch traced here: 73.9 us
  Pallas kernels  72 us (97%)
  local copies, waits for them, and re-layouts  1.8 us (2%)
    pallas_call x1, Pallas kernels, step(): pl.pallas_call(functools.partial(kernel, peers, group_len, factor), out_s...  72 us
    unnamed x3, local copies, waits for them, and re-layouts  1.8 us

profile of v3, /device:TPU:6, one launch (start us, length us, event | category | flops | bytes accessed | tf_op | source)
XLA Modules:
  0.0 73.9 jit_solution(2930981825615088205)
XLA Ops:
  0.0 0.0 copy-start
  0.0 1.0 %copy-done = bf16[16,16384]{1,0:T(8,128)(2,1)S(1)} copy-done((bf16[16,16384]{1,0:T(8,128)(2,1)S(1)}, bf16[16,16384]{1,0:T(8,128)(2,1)}, u32[]{:S(2)}) %copy-start) | copy-done | bytes 524312
  1.0 72.0 %shard_map.28 = f32[1,416,256]{2,1,0:T(8,128)S(1)} custom-call(bf16[16,53248]{1,0:T(8,128)(2,1)} %act_hbm.1, bf16[16,16384]{1,0:T(8,128)(2,1)S(1)} %copy-done), custom_call_target="tpu_custom_call" | custom-call | tf_op jit(solution)/shard_map/pallas_call | solution.py:381
  73.1 0.8 %copy.4 = f32[1,256,416]{1,2,0:T(8,128)} copy(f32[1,256,416]{1,2,0:T(8,128)S(1)} %bitcast.1) | data formatting | bytes 851968
Async XLA Ops:
  0.0 1.0 %copy-start = (bf16[16,16384]{1,0:T(8,128)(2,1)S(1)}, bf16[16,16384]{1,0:T(8,128)(2,1)}, u32[]{:S(2)}) copy-start(bf16[16,16384]{1,0:T(8,128)(2,1)} %grads_hbm.1) | copy-start | bytes 1572868
